TPU v7x, 128 devices: a whole 4x4x4 slice. The times are simulated.
128 devices in a mesh: batch: 128 (over x, y, z, core).
Axes of the slice: x: 4, y: 4, z: 4, core: 2. Of those that a mesh axis runs over, the one named last changes fastest.
Arguments:
- images: bfloat16 [65536, 1152], P('batch'), may hold values from -6 to 6
- texts: bfloat16 [65536, 1152], P('batch'), may hold values from -6 to 6
Outputs:
- row_loss: float32 [65536], P('batch')
- grad_images: float32 [65536, 1152], P('batch')
- grad_texts: float32 [65536, 1152], P('batch')
All inputs are finite; a program needn't handle non-finite values.
Results may differ from a plain program's by a relative error of at most 0.0018.
Values may be sent and summed in bfloat16 or wider, within the bound.
A program may use at most 128 MiB of HBM per device.

v0:
```python
import math

import jax
import jax.numpy as jnp
from jax import lax
from jax.sharding import PartitionSpec as P

SECTIONS = 3


def from_partner(value, axis, bit):
    mask = 2**bit
    pairs = [(source, source ^ mask) for source in range(lax.axis_size(axis))]
    return lax.ppermute(value, axis, pairs)


def join_blocks(held, arrived, upper):
    return jnp.where(
        upper == 1, jnp.concatenate([arrived, held], 0), jnp.concatenate([held, arrived], 0)
    )


def coef_rows(sliced, images):
    return lax.dot_general(
        sliced, images, (((0,), (0,)), ((), ())), preferred_element_type=jnp.float32
    )


def per_device(images, texts):
    rows = images.shape[0]
    width = images.shape[1]
    members = 2**SECTIONS
    group_rows = rows * members
    scale = 2.0 / math.sqrt(width)
    stride = lax.axis_size("batch") // members
    base_bit = stride.bit_length() - 1
    device = lax.axis_index("batch")
    member = device >> base_bit
    held_texts = texts
    for level in range(SECTIONS):
        arrived_texts = from_partner(held_texts, "batch", base_bit + level)
        upper = member >> level & 1
        held_texts = join_blocks(held_texts, arrived_texts, upper)
    logits = (
        lax.dot_general(
            images, held_texts, (((1,), (1,)), ((), ())), preferred_element_type=jnp.float32
        )
        * scale
        - 1.0
    )
    columns = lax.broadcasted_iota(jnp.int32, (rows, group_rows), 1)
    own_rows = lax.broadcasted_iota(jnp.int32, (rows, group_rows), 0) + member * rows
    match = columns == own_rows
    signed = jnp.where(match, logits, -logits)
    row_loss = jnp.mean(-jax.nn.log_sigmoid(signed), axis=1)
    coef = (scale * (jax.nn.sigmoid(logits) - match.astype(jnp.float32))).astype(jnp.bfloat16)
    grad_images = jnp.dot(coef, held_texts, preferred_element_type=jnp.float32)
    partial_value = None
    span = group_rows
    for level in reversed(range(SECTIONS)):
        half_rows = span // 2
        upper = member >> level & 1
        if partial_value is None:
            far_coef = lax.dynamic_slice_in_dim(coef, (1 - upper) * half_rows, half_rows, 1)
            near_coef = lax.dynamic_slice_in_dim(coef, upper * half_rows, half_rows, 1)
            outgoing = coef_rows(far_coef, images)
            kept = coef_rows(near_coef, images)
        else:
            outgoing = lax.dynamic_slice_in_dim(
                partial_value, (1 - upper) * half_rows, half_rows, 0
            )
            kept = lax.dynamic_slice_in_dim(partial_value, upper * half_rows, half_rows, 0)
        arrived = from_partner(outgoing, "batch", base_bit + level)
        partial_value = arrived + kept
        span = half_rows
    return (row_loss, grad_images, partial_value)


def solution(mesh):
    placed = (P("batch", None), P("batch", None))
    return jax.shard_map(
        per_device,
        mesh=mesh,
        in_specs=placed,
        out_specs=(P("batch"), P("batch", None), P("batch", None)),
        check_vma=False,
    )
```

profile of v0, /device:TPU:0, one launch (start us, length us, event | category | flops | bytes accessed | tf_op | source)
XLA Modules:
  0.0 597.2 jit_solution(14811219639428511102)
XLA Ops:
  0.6 0.0 copy-start
  0.6 3.4 collective-permute-start
  4.0 26.3 %collective-permute-done = bf16[512,1152]{1,0:T(8,128)(2,1)} collective-permute-done((bf16[512,1152]{1,0:T(8,128)(2,1)}, bf16[512,1152]{1,0:T(8,128)(2,1)}, u32[]{:S(2)}, u32[]{:S(2)}) %collective-permute-start) | collective-permute-done | bytes 1179680 | tf_op jit(solution)/shard_map/ppermute | solution.py:14
  30.3 3.0 maximum_select_fusion.2
  33.2 1.6 collective-permute-start.1
  34.9 50.7 %collective-permute-done.1 = bf16[1024,1152]{1,0:T(8,128)(2,1)} collective-permute-done((bf16[1024,1152]{1,0:T(8,128)(2,1)S(1)}, bf16[1024,1152]{1,0:T(8,128)(2,1)}, u32[]{:S(2)}, u32[]{:S(2)}) %collective-permute-start.1) | collective-permute-done | bytes 2359328 | tf_op jit(solution)/shard_map/ppermute | solution.py:14
  85.6 6.0 %maximum_select_fusion.1 = bf16[2048,1152]{1,0:T(8,128)(2,1)} fusion(bf16[1024,1152]{1,0:T(8,128)(2,1)S(1)} %maximum_select_fusion.2, bf16[1024,1152]{1,0:T(8,128)(2,1)} %collective-permute-done.1, pred[]{:T(512)S(6)} %eq.14), kind=kLoop, calls=%fused_computation.14 | loop fusion | flops 21233664 | bytes 9437185 | tf_op jit(solution)/shard_map/jit(_where)/select_n | solution.py:18
  91.6 3.0 collective-permute-start.2
  94.6 100.6 %collective-permute-done.2 = bf16[2048,1152]{1,0:T(8,128)(2,1)} collective-permute-done((bf16[2048,1152]{1,0:T(8,128)(2,1)}, bf16[2048,1152]{1,0:T(8,128)(2,1)}, u32[]{:S(2)}, u32[]{:S(2)}) %collective-permute-start.2) | collective-permute-done | bytes 4718624 | tf_op jit(solution)/shard_map/ppermute | solution.py:14
  195.2 0.0 copy-done
  195.2 20.3 %fusion.6 = (bf16[512,4096]{0,1:T(8,128)(2,1)S(1)}, f32[512]{0:T(512)S(1)}) fusion(s32[512]{0:T(512)S(1)} %iota_add_fusion, bf16[512,1152]{1,0:T(8,128)(2,1)S(1)} %copy-done, bf16[2048,1152]{1,0:T(8,128)(2,1)} %maximum_select_fusion.1, bf16[2048,1152]{1,0:T(8,128)(2,1)} %collective-permute-done.2, pred[]{:T(512)S(6)} %eq.13), kind=kOutput, calls=%fused_computation.13 | convolution fusion | flops 4914150912 | bytes 14815233 | tf_op jit(solution)/shard_map/dot_general | solution.py:45
  215.5 0.0 copy-start.5
  215.5 5.3 fusion.8
  220.8 0.0 copy-done.5
  220.8 3.0 collective-permute-start.3
  223.8 200.8 %collective-permute-done.3 = f32[2048,1152]{1,0:T(8,128)} collective-permute-done((f32[2048,1152]{1,0:T(8,128)}, f32[2048,1152]{1,0:T(8,128)}, u32[]{:S(2)}, u32[]{:S(2)}) %collective-permute-start.3) | collective-permute-done | bytes 9437216 | tf_op jit(solution)/shard_map/ppermute | solution.py:14
  424.6 7.5 %convolution_add_fusion = f32[2048,1152]{1,0:T(8,128)S(1)} fusion(f32[2048,1152]{1,0:T(8,128)} %collective-permute-done.3, bf16[512,1152]{1,0:T(8,128)(2,1)S(1)} %copy-done, bf16[512,4096]{0,1:T(8,128)(2,1)} %copy-done.5, s32[]{:T(128)S(6)} %select_n.60), kind=kOutput, calls=%fused_computation.4 | convolution fusion | flops 2418278400 | bytes 22151172 | tf_op jit(solution)/shard_map/dot_general | solution.py:24
  432.1 0.0 copy-start.2
  432.1 2.7 constant_dynamic-slice_fusion.1
  434.8 2.4 copy-done.2
  437.1 1.4 collective-permute-start.4
  438.6 98.8 %collective-permute-done.4 = f32[1024,1152]{1,0:T(8,128)} collective-permute-done((f32[1024,1152]{1,0:T(8,128)}, f32[1024,1152]{1,0:T(8,128)}, u32[]{:S(2)}, u32[]{:S(2)}) %collective-permute-start.4) | collective-permute-done | bytes 4718624 | tf_op jit(solution)/shard_map/ppermute | solution.py:14
  537.4 4.2 dynamic-slice_add_fusion
  541.7 0.0 copy-start.3
  541.7 2.1 copy-done.3
  543.8 1.6 constant_dynamic-slice_fusion
  545.4 3.1 collective-permute-start.5
  548.4 0.6 broadcast_multiply_fusion
  549.0 0.0 copy-start.4
  549.0 0.0 copy-start.1
  549.0 13.1 %fusion.10 = f32[512,1152]{1,0:T(8,128)} fusion(bf16[512,4096]{0,1:T(8,128)(2,1)} %copy-done.5, bf16[2048,1152]{1,0:T(8,128)(2,1)} %maximum_select_fusion.1, bf16[2048,1152]{1,0:T(8,128)(2,1)} %collective-permute-done.2, pred[]{:T(512)S(6)} %eq.13), kind=kOutput, calls=%fused_computation.21 | convolution fusion | flops 4874305536 | bytes 15990785 | tf_op jit(solution)/shard_map/dot_general | solution.py:57
  562.2 33.4 %collective-permute-done.5 = f32[512,1152]{1,0:T(8,128)S(1)} collective-permute-done((f32[512,1152]{1,0:T(8,128)}, f32[512,1152]{1,0:T(8,128)S(1)}, u32[]{:S(2)}, u32[]{:S(2)}) %collective-permute-start.5) | collective-permute-done | bytes 2359328 | tf_op jit(solution)/shard_map/ppermute | solution.py:14
  595.5 0.0 copy-done.4
  595.5 1.6 dynamic-slice_add_fusion.1
  597.2 0.0 copy-done.1
  (1 shorter events, 0.0 us)
Async XLA Ops:
  0.6 194.5 %copy-start = (bf16[512,1152]{1,0:T(8,128)(2,1)S(1)}, bf16[512,1152]{1,0:T(8,128)(2,1)}, u32[]{:S(2)}) copy-start(bf16[512,1152]{1,0:T(8,128)(2,1)} %param.2) | copy-start | bytes 3538948
  0.6 29.6 %collective-permute-start = (bf16[512,1152]{1,0:T(8,128)(2,1)}, bf16[512,1152]{1,0:T(8,128)(2,1)}, u32[]{:S(2)}, u32[]{:S(2)}) collective-permute-start(bf16[512,1152]{1,0:T(8,128)(2,1)} %param.3), channel_id=1, source_target_pairs={{0,16},{1,17},{2,18},{3,19},{4,20},{5,21},{6,22},{7,23},{8,24},{9,... | collective-permute-start | bytes 3538952 | tf_op jit(solution)/shard_map/ppermute | solution.py:14
  33.2 52.3 %collective-permute-start.1 = (bf16[1024,1152]{1,0:T(8,128)(2,1)S(1)}, bf16[1024,1152]{1,0:T(8,128)(2,1)}, u32[]{:S(2)}, u32[]{:S(2)}) collective-permute-start(bf16[1024,1152]{1,0:T(8,128)(2,1)S(1)} %maximum_select_fusion.2), channel_id=1, source_target_pairs={{0,32},{1,33},{2,34},{3,35},{4,36},{5,37},{6,38},{7,39},{8,40},{9,... | collective-permute-start | bytes 7077896 | tf_op jit(solution)/shard_map/ppermute | solution.py:14
  91.6 103.6 %collective-permute-start.2 = (bf16[2048,1152]{1,0:T(8,128)(2,1)}, bf16[2048,1152]{1,0:T(8,128)(2,1)}, u32[]{:S(2)}, u32[]{:S(2)}) collective-permute-start(bf16[2048,1152]{1,0:T(8,128)(2,1)} %maximum_select_fusion.1), channel_id=1, source_target_pairs={{0,64},{1,65},{2,66},{3,67},{4,68},{5,69},{6,70},{7,71},{8,72},{9,... | collective-permute-start | bytes 14155784 | tf_op jit(solution)/shard_map/ppermute | solution.py:14
  215.5 5.3 copy-start.5
  220.8 203.8 %collective-permute-start.3 = (f32[2048,1152]{1,0:T(8,128)}, f32[2048,1152]{1,0:T(8,128)}, u32[]{:S(2)}, u32[]{:S(2)}) collective-permute-start(f32[2048,1152]{1,0:T(8,128)} %fusion.8), channel_id=1, source_target_pairs={{0,64},{1,65},{2,66},{3,67},{4,68},{5,69},{6,70},{7,71},{8,72},{9,... | collective-permute-start | bytes 28311560 | tf_op jit(solution)/shard_map/ppermute | solution.py:14
  432.1 5.0 copy-start.2
  437.1 100.3 %collective-permute-start.4 = (f32[1024,1152]{1,0:T(8,128)}, f32[1024,1152]{1,0:T(8,128)}, u32[]{:S(2)}, u32[]{:S(2)}) collective-permute-start(f32[1024,1152]{1,0:T(8,128)} %constant_dynamic-slice_fusion.1), channel_id=1, source_target_pairs={{0,32},{1,33},{2,34},{3,35},{4,36},{5,37},{6,38},{7,39},{8,40},{9,... | collective-permute-start | bytes 14155784 | tf_op jit(solution)/shard_map/ppermute | solution.py:14
  541.7 2.1 copy-start.3
  545.4 50.2 %collective-permute-start.5 = (f32[512,1152]{1,0:T(8,128)}, f32[512,1152]{1,0:T(8,128)S(1)}, u32[]{:S(2)}, u32[]{:S(2)}) collective-permute-start(f32[512,1152]{1,0:T(8,128)} %constant_dynamic-slice_fusion), channel_id=1, source_target_pairs={{0,16},{1,17},{2,18},{3,19},{4,20},{5,21},{6,22},{7,23},{8,24},{9,... | collective-permute-start | bytes 7077896 | tf_op jit(solution)/shard_map/ppermute | solution.py:14
  549.0 46.5 %copy-start.4 = (f32[1024,1152]{1,0:T(8,128)S(1)}, f32[1024,1152]{1,0:T(8,128)}, u32[]{:S(2)}) copy-start(f32[1024,1152]{1,0:T(8,128)} %copy-done.3) | copy-start | bytes 14155780
  549.0 48.2 %copy-start.1 = (bf16[512,1152]{1,0:T(8,128)(2,1)S(1)}, bf16[512,1152]{1,0:T(8,128)(2,1)}, u32[]{:S(2)}) copy-start(bf16[512,1152]{1,0:T(8,128)(2,1)} %param.2) | copy-start | bytes 3538948
where the time goes:
time: 597 us
  waiting for transfers between devices  511 us (86%)
  matrix products  46.2 us (8%)
  starting transfers between devices  15.5 us (3%)
  other arithmetic  15.4 us (3%)
  local copies, waits for them, and re-layouts  8.76 us (1%)
    ppermute x6, waiting for transfers between devices, from_partner(): return lax.ppermute(value, axis, pairs)  511 us
    dot_general x1, matrix products, per_device(): lax.dot_general(images, held_texts, (((1,), (1,)), ((), ())), preferred_e...  20.3 us
    ppermute x6, starting transfers between devices, from_partner(): return lax.ppermute(value, axis, pairs)  15.5 us
    dot_general x1, matrix products, per_device(): grad_images = jnp.dot(coef, held_texts, preferred_element_type=jnp.float32)  13.1 us
    dot_general x2, matrix products, coef_rows(): lax.dot_general(sliced, images, (((0,), (0,)), ((), ())), preferred_eleme...  12.8 us
  transfers between devices with their start and end apart: 6, of which 6 were waited for; matrix products, arithmetic and copies ran while one was open for 2% of the time, Pallas kernels for 0%

commit v1 on v0

v1 whole, which is shorter than its diff:
```python
import functools
import math

import jax
import jax.numpy as jnp
from jax import lax
from jax.experimental import pallas as pl
from jax.experimental.pallas import tpu as pltpu
from jax.sharding import PartitionSpec as P

MESH = pl.DeviceIdType.MESH
F32 = jnp.float32
BF16 = jnp.bfloat16
OWN, YP, AP, FAR = 0, 1, 2, 3
CHUNK = 128
HALF = 256


def pair_terms(products, scale, match):
    logits = products * scale - 1.0
    small = jnp.exp(-jnp.abs(logits))
    inverse = 1.0 / (1.0 + small)
    sig = jnp.where(logits >= 0.0, inverse, small * inverse)
    tail = jnp.where(
        small < 1e-2,
        small * (1.0 - small * (0.5 - small * (1.0 / 3.0))),
        jnp.log(1.0 + small),
    )
    if match is None:
        return (scale * sig).astype(BF16), jnp.maximum(logits, 0.0) + tail
    coef = (scale * (sig - match.astype(F32))).astype(BF16)
    return coef, jnp.maximum(jnp.where(match, -logits, logits), 0.0) + tail


def kernel(
    images, texts, row_loss, grad_images, grad_texts,
    im, tx, coef, losses, far_losses, grad_b, hold,
    out_y, out_a, out_far, out_b, in_y, in_a, in_far, in_b,
    send, recv, local,
):
    rows, width = images.shape
    scale = 2.0 / math.sqrt(width)
    me = lax.axis_index("batch")
    core = lax.rem(me, 2)
    x = lax.div(me, 32)
    near = me + 32 * (1 - 2 * lax.rem(x, 2))
    other = me + 32 * (3 - 2 * x)
    a = near * (1 - core) + other * core
    b = other * (1 - core) + near * core
    y = me + 16 * (1 - 2 * lax.rem(lax.div(me, 16), 2))

    count = [0]

    def to(src, dst, device):
        k = count[0]
        count[0] += 1
        return pltpu.make_async_remote_copy(
            src, dst, send.at[k], recv.at[k], device_id=(device,), device_id_type=MESH
        )

    chunks = [pl.ds(k * CHUNK, CHUNK) for k in range(rows // CHUNK)]
    image_b = [to(images.at[c], im.at[pl.ds(rows + c.start, CHUNK)], b) for c in chunks]
    text_y = [to(texts.at[c], tx.at[YP, c], y) for c in chunks]
    text_a = [to(texts.at[c], tx.at[AP, c], a) for c in chunks]
    text_far = [
        to(tx.at[AP, c], tx.at[FAR, c], y) if c.start < CHUNK else to(tx.at[YP, c], tx.at[FAR, c], a)
        for c in chunks
    ]
    back_far = [
        to(out_far.at[c], in_far.at[c], y if c.start < CHUNK else a) for c in chunks
    ]
    back_y = [to(out_y.at[c], in_y.at[c], y) for c in chunks]
    back_a = [to(out_a.at[c], in_a.at[c], a) for c in chunks]
    back_b = [to(out_b.at[c], in_b.at[c], b) for c in chunks]
    back_loss = to(losses.at[1], far_losses, b)

    barrier = pltpu.get_barrier_semaphore()
    for device in (a, b, y):
        pl.semaphore_signal(barrier, inc=1, device_id=(device,), device_id_type=MESH)
    pl.semaphore_wait(barrier, 3)

    for copy in image_b + text_y:
        copy.start()
    own_text = pltpu.make_async_copy(texts, tx.at[OWN], local.at[0])
    own_image = pltpu.make_async_copy(images, im.at[pl.ds(0, rows)], local.at[1])
    own_text.start()
    own_image.start()
    own_text.wait()
    own_image.wait()

    def pairs(slot, first, size, side, diagonal):
        columns = pl.ds(side * rows, rows)
        products = lax.dot_general(
            tx[slot, first:first + size], im[columns], (((1,), (1,)), ((), ())),
            preferred_element_type=F32,
        )
        match = None
        if diagonal:
            match = lax.broadcasted_iota(jnp.int32, (size, rows), 0) == (
                lax.broadcasted_iota(jnp.int32, (size, rows), 1)
            )
        c, loss = pair_terms(products, scale, match)
        coef[:size, columns] = c
        part = loss.reshape(size // 8, 8, rows).sum(0)
        losses[side] = part if slot == OWN else losses[side] + part

    def text_part(size):
        return jnp.dot(coef[:size], im[...], preferred_element_type=F32)

    def image_part(slot, first, size, side):
        return lax.dot_general(
            coef[:size, side * rows:(side + 1) * rows], tx[slot, first:first + size],
            (((0,), (0,)), ((), ())), preferred_element_type=F32,
        )

    def step(slot, first, size):
        for side in (0, 1):
            pairs(slot, first, size, side, False)

    pairs(OWN, 0, rows, 0, True)
    for copy in image_b:
        copy.wait()
    for copy in text_a:
        copy.start()
    pairs(OWN, 0, rows, 1, False)
    grad_texts[...] = text_part(rows)
    grad_images[...] = image_part(OWN, 0, rows, 0)
    grad_b[...] = image_part(OWN, 0, rows, 1)

    for k in (0, 1):
        text_y[k].wait()
    text_far[1].start()
    step(YP, 0, HALF)
    part = text_part(HALF)
    out_y[:CHUNK] = part[:CHUNK].astype(BF16)
    hold[CHUNK:HALF] = part[CHUNK:]
    grad_images[...] += image_part(YP, 0, HALF, 0)
    grad_b[...] += image_part(YP, 0, HALF, 1)

    for k in (0, 1):
        text_a[k].wait()
    text_far[0].start()
    step(AP, 0, HALF)
    part = text_part(HALF)
    hold[:CHUNK] = part[:CHUNK]
    out_a[CHUNK:HALF] = part[CHUNK:].astype(BF16)
    grad_images[...] += image_part(AP, 0, HALF, 0)
    grad_b[...] += image_part(AP, 0, HALF, 1)

    for k in (2, 3):
        text_y[k].wait()
        text_far[k].start()
    step(YP, HALF, HALF)
    hold[HALF:] = text_part(HALF)
    grad_images[...] += image_part(YP, HALF, HALF, 0)
    grad_b[...] += image_part(YP, HALF, HALF, 1)

    for k in (2, 3):
        text_a[k].wait()
    step(AP, HALF, HALF)
    out_a[HALF:] = text_part(HALF).astype(BF16)
    grad_images[...] += image_part(AP, HALF, HALF, 0)
    grad_b[...] += image_part(AP, HALF, HALF, 1)
    back_y[0].start()
    for k in (1, 2, 3):
        back_a[k].start()

    for k in (0, 1):
        text_far[k].wait()
    step(FAR, 0, HALF)
    out_far[:HALF] = text_part(HALF).astype(BF16)
    for k in (0, 1):
        back_far[k].start()
    grad_images[...] += image_part(FAR, 0, HALF, 0)
    grad_b[...] += image_part(FAR, 0, HALF, 1)

    for k in (2, 3):
        text_far[k].wait()
    step(FAR, HALF, HALF)
    back_loss.start()
    out_far[HALF:] = text_part(HALF).astype(BF16)
    for k in (2, 3):
        back_far[k].start()
    out_b[...] = (grad_b[...] + image_part(FAR, HALF, HALF, 1)).astype(BF16)
    for copy in back_b:
        copy.start()
    grad_images[...] += image_part(FAR, HALF, HALF, 0)

    for k, c in enumerate(chunks):
        back_far[k].wait()
        out = out_a if k == 0 else out_y
        out[c] = (hold[c] + in_far[c].astype(F32)).astype(BF16)
        (back_a if k == 0 else back_y)[k].start()
    back_loss.wait()
    row_loss[...] = jnp.sum(losses[0] + far_losses[...], axis=0, keepdims=True) * (1.0 / (8 * rows))
    for k, c in enumerate(chunks):
        back_a[k].wait()
        back_y[k].wait()
        grad_texts[c] += in_a[c].astype(F32) + in_y[c].astype(F32)
    for k, c in enumerate(chunks):
        back_b[k].wait()
        grad_images[c] += in_b[c].astype(F32)


def per_device(images, texts):
    rows, width = images.shape
    block = (rows, width)
    copies = 8 * (rows // CHUNK) + 1
    loss, grad_images, grad_texts = pl.pallas_call(
        kernel,
        out_shape=(
            jax.ShapeDtypeStruct((1, rows), F32),
            jax.ShapeDtypeStruct(block, F32),
            jax.ShapeDtypeStruct(block, F32),
        ),
        in_specs=[pl.BlockSpec(memory_space=pl.ANY)] * 2,
        out_specs=(pl.BlockSpec(memory_space=pltpu.VMEM),) * 3,
        scratch_shapes=[
            pltpu.VMEM((2 * rows, width), BF16),
            pltpu.VMEM((4, rows, width), BF16),
            pltpu.VMEM((rows, 2 * rows), BF16),
            pltpu.VMEM((2, 8, rows), F32),
            pltpu.VMEM((8, rows), F32),
            pltpu.VMEM(block, F32),
            pltpu.VMEM(block, F32),
        ]
        + [pltpu.VMEM(block, BF16)] * 8
        + [
            pltpu.SemaphoreType.DMA((copies,)),
            pltpu.SemaphoreType.DMA((copies,)),
            pltpu.SemaphoreType.DMA((2,)),
        ],
        compiler_params=pltpu.CompilerParams(
            collective_id=0, has_side_effects=True, vmem_limit_bytes=56 * 2**20
        ),
        cost_estimate=pl.CostEstimate(
            flops=6 * 8 * rows * rows * width, bytes_accessed=12 * rows * width,
            transcendentals=3 * 8 * rows * rows,
        ),
    )(images, texts)
    return loss.reshape(rows), grad_images, grad_texts


def solution(mesh):
    placed = (P("batch", None), P("batch", None))
    return jax.shard_map(
        per_device,
        mesh=mesh,
        in_specs=placed,
        out_specs=(P("batch"), P("batch", None), P("batch", None)),
        check_vma=False,
    )
```

time: 597 us -> 95.2 us (0.16)
  waiting for transfers between devices: 511 us -> 0 us
  Pallas kernels: 0 us -> 88.4 us
  matrix products: 46.2 us -> 0 us
  starting transfers between devices: 15.5 us -> 0 us
  other arithmetic: 15.4 us -> 0 us
    ppermute x6 -> x0, waiting for transfers between devices: 511 us -> none  [from_partner(): return lax.ppermute(value, axis, pairs)]
    pallas_call x0 -> x1, Pallas kernels: none -> 88.4 us  [per_device(): pl.pallas_call(kernel, out_shape=(jax.ShapeDtypeStruct((1, rows), F32), j...]
    dot_general x4 -> x0, matrix products: 46.2 us -> none  [the longest x1 20.3 us: per_device(): lax.dot_general(images, held_texts, (((1,), (1,)), ((), ())), preferred_e...]
    ppermute x6 -> x0, starting transfers between devices: 15.5 us -> none  [from_partner(): return lax.ppermute(value, axis, pairs)]
    select_n x2 -> x0, other arithmetic: 8.93 us -> none  [join_blocks(): jnp.where(upper == 1, jnp.concatenate([arrived, held], 0), jnp.concatenat...]
  transfers between devices with their start and end apart: 6 -> 0, of which waited for: 6 -> 0; matrix products, arithmetic and copies ran while one was open for 2% -> 0% of each run, Pallas kernels for 0% -> 0%
where the time goes in v1:
time: 95.2 us; the launch traced here: 95.1 us
  Pallas kernels  88.4 us (93%)
  local copies, waits for them, and re-layouts  6.03 us (6%)
    pallas_call x1, Pallas kernels, per_device(): pl.pallas_call(kernel, out_shape=(jax.ShapeDtypeStruct((1, rows), F32), j...  88.4 us
    unnamed x5, local copies, waits for them, and re-layouts  6.03 us

profile of v1, /device:TPU:0, one launch (start us, length us, event | category | flops | bytes accessed | tf_op | source)
XLA Modules:
  0.0 95.1 jit_solution(18268271938743779608)
XLA Ops:
  0.6 88.4 %shard_map.49 = (f32[1,512]{1,0:T(1,128)}, f32[512,1152]{1,0:T(8,128)}, f32[512,1152]{1,0:T(8,128)}) custom-call(bf16[512,1152]{1,0:T(8,128)(2,1)} %images.1, bf16[512,1152]{1,0:T(8,128)(2,1)} %texts.1), custom_call_target="tpu_custom_call" | custom-call | flops 14495514624 | bytes 7077888 | tf_op jit(solution)/shard_map/pallas_call | solution.py:209
  89.0 1.3 %copy.8 = f32[512]{0:T(512)} copy(f32[512]{0:T(512)} %bitcast.1) | data formatting | bytes 4096
  90.3 0.0 copy-start
  90.3 3.4 %copy.9 = f32[512,1152]{1,0:T(8,128)} copy(f32[512,1152]{1,0:T(8,128)} %get-tuple-element.13) | data formatting | bytes 4718592
  93.6 0.0 copy-done
  93.7 1.4 %copy.10 = f32[512,1152]{1,0:T(8,128)} copy(f32[512,1152]{1,0:T(8,128)S(1)} %copy-done) | data formatting | bytes 4718592
Async XLA Ops:
  90.3 3.4 %copy-start = (f32[512,1152]{1,0:T(8,128)S(1)}, f32[512,1152]{1,0:T(8,128)}, u32[]{:S(2)}) copy-start(f32[512,1152]{1,0:T(8,128)} %get-tuple-element.14) | copy-start | bytes 7077892

commit v2 on v1

--- a/solution.py
+++ b/solution.py
@@ -79,8 +79,18 @@
         pl.semaphore_signal(barrier, inc=1, device_id=(device,), device_id_type=MESH)
     pl.semaphore_wait(barrier, 3)
 
-    for copy in image_b + text_y:
-        copy.start()
+    started = []
+
+    def start(*copies):
+        for copy in copies:
+            copy.start()
+            started.append(copy)
+
+    def arrived(*copies):
+        for copy in copies:
+            copy.wait_recv()
+
+    start(*image_b, *text_y)
     own_text = pltpu.make_async_copy(texts, tx.at[OWN], local.at[0])
     own_image = pltpu.make_async_copy(images, im.at[pl.ds(0, rows)], local.at[1])
     own_text.start()
@@ -88,7 +98,7 @@
     own_text.wait()
     own_image.wait()
 
-    def pairs(slot, first, size, side, diagonal):
+    def pairs(slot, first, size, side, diagonal=False):
         columns = pl.ds(side * rows, rows)
         products = lax.dot_general(
             tx[slot, first:first + size], im[columns], (((1,), (1,)), ((), ())),
@@ -113,105 +123,116 @@
             (((0,), (0,)), ((), ())), preferred_element_type=F32,
         )
 
-    def step(slot, first, size):
-        for side in (0, 1):
-            pairs(slot, first, size, side, False)
+    def both_pairs(slot, first):
+        pairs(slot, first, HALF, 0)
+        pairs(slot, first, HALF, 1)
+
+    def both_images(slot, first):
+        grad_images[...] += image_part(slot, first, HALF, 0)
+        grad_b[...] += image_part(slot, first, HALF, 1)
 
     pairs(OWN, 0, rows, 0, True)
-    for copy in image_b:
-        copy.wait()
-    for copy in text_a:
-        copy.start()
-    pairs(OWN, 0, rows, 1, False)
+    image_b[2].wait_send()
+    start(text_a[0])
+    image_b[3].wait_send()
+    start(*text_a[1:])
+    arrived(*image_b)
+    pairs(OWN, 0, rows, 1)
     grad_texts[...] = text_part(rows)
     grad_images[...] = image_part(OWN, 0, rows, 0)
     grad_b[...] = image_part(OWN, 0, rows, 1)
 
-    for k in (0, 1):
-        text_y[k].wait()
-    text_far[1].start()
-    step(YP, 0, HALF)
+    arrived(text_y[0], text_y[1])
+    both_pairs(YP, 0)
     part = text_part(HALF)
     out_y[:CHUNK] = part[:CHUNK].astype(BF16)
     hold[CHUNK:HALF] = part[CHUNK:]
-    grad_images[...] += image_part(YP, 0, HALF, 0)
-    grad_b[...] += image_part(YP, 0, HALF, 1)
-
-    for k in (0, 1):
-        text_a[k].wait()
-    text_far[0].start()
-    step(AP, 0, HALF)
+    start(text_far[1])
+    both_images(YP, 0)
+
+    arrived(text_a[0], text_a[1])
+    both_pairs(AP, 0)
     part = text_part(HALF)
     hold[:CHUNK] = part[:CHUNK]
     out_a[CHUNK:HALF] = part[CHUNK:].astype(BF16)
-    grad_images[...] += image_part(AP, 0, HALF, 0)
-    grad_b[...] += image_part(AP, 0, HALF, 1)
-
-    for k in (2, 3):
-        text_y[k].wait()
-        text_far[k].start()
-    step(YP, HALF, HALF)
+    both_images(AP, 0)
+
+    arrived(text_y[2])
+    start(text_far[2], text_far[0])
+    arrived(text_y[3])
+    start(text_far[3])
+    both_pairs(YP, HALF)
     hold[HALF:] = text_part(HALF)
-    grad_images[...] += image_part(YP, HALF, HALF, 0)
-    grad_b[...] += image_part(YP, HALF, HALF, 1)
-
-    for k in (2, 3):
-        text_a[k].wait()
-    step(AP, HALF, HALF)
+    both_images(YP, HALF)
+
+    arrived(text_a[2], text_a[3])
+    both_pairs(AP, HALF)
     out_a[HALF:] = text_part(HALF).astype(BF16)
-    grad_images[...] += image_part(AP, HALF, HALF, 0)
-    grad_b[...] += image_part(AP, HALF, HALF, 1)
-    back_y[0].start()
-    for k in (1, 2, 3):
-        back_a[k].start()
-
-    for k in (0, 1):
-        text_far[k].wait()
-    step(FAR, 0, HALF)
+    start(back_y[0])
+    both_images(AP, HALF)
+
+    arrived(text_far[0], text_far[1])
+    both_pairs(FAR, 0)
     out_far[:HALF] = text_part(HALF).astype(BF16)
-    for k in (0, 1):
-        back_far[k].start()
-    grad_images[...] += image_part(FAR, 0, HALF, 0)
-    grad_b[...] += image_part(FAR, 0, HALF, 1)
-
-    for k in (2, 3):
-        text_far[k].wait()
-    step(FAR, HALF, HALF)
-    back_loss.start()
+    start(back_far[1], back_far[0])
+    both_images(FAR, 0)
+    arrived(text_far[2], text_far[3])
+    start(back_a[1], back_a[2])
+    both_pairs(FAR, HALF)
+    start(back_loss)
     out_far[HALF:] = text_part(HALF).astype(BF16)
-    for k in (2, 3):
-        back_far[k].start()
+    start(back_far[2], back_far[3])
     out_b[...] = (grad_b[...] + image_part(FAR, HALF, HALF, 1)).astype(BF16)
-    for copy in back_b:
-        copy.start()
     grad_images[...] += image_part(FAR, HALF, HALF, 0)
 
-    for k, c in enumerate(chunks):
-        back_far[k].wait()
-        out = out_a if k == 0 else out_y
+    def pass_on(k):
+        out, back = (out_a, back_a) if k == 0 else (out_y, back_y)
+        c = chunks[k]
+        arrived(back_far[k])
         out[c] = (hold[c] + in_far[c].astype(F32)).astype(BF16)
-        (back_a if k == 0 else back_y)[k].start()
-    back_loss.wait()
+        start(back[k])
+
+    pass_on(1)
+    start(back_a[3], back_b[0])
+    pass_on(2)
+    start(*back_b[1:])
+    pass_on(3)
+    pass_on(0)
+    arrived(back_loss)
     row_loss[...] = jnp.sum(losses[0] + far_losses[...], axis=0, keepdims=True) * (1.0 / (8 * rows))
-    for k, c in enumerate(chunks):
-        back_a[k].wait()
-        back_y[k].wait()
+    for k in (1, 2, 3, 0):
+        c = chunks[k]
+        arrived(back_a[k], back_y[k])
         grad_texts[c] += in_a[c].astype(F32) + in_y[c].astype(F32)
     for k, c in enumerate(chunks):
-        back_b[k].wait()
+        arrived(back_b[k])
         grad_images[c] += in_b[c].astype(F32)
+    for copy in started:
+        if copy is not image_b[2] and copy is not image_b[3]:
+            copy.wait_send()
+
+
+def write_out(*refs):
+    sources, targets, done = refs[:3], refs[3:6], refs[6]
+    copies = [pltpu.make_async_copy(s, t, done.at[k]) for k, (s, t) in enumerate(zip(sources, targets))]
+    for copy in copies:
+        copy.start()
+    for copy in copies:
+        copy.wait()
 
 
 def per_device(images, texts):
+    images = pltpu.with_memory_space_constraint(images, pltpu.HBM)
+    texts = pltpu.with_memory_space_constraint(texts, pltpu.HBM)
     rows, width = images.shape
     block = (rows, width)
     copies = 8 * (rows // CHUNK) + 1
-    loss, grad_images, grad_texts = pl.pallas_call(
+    results = pl.pallas_call(
         kernel,
         out_shape=(
-            jax.ShapeDtypeStruct((1, rows), F32),
-            jax.ShapeDtypeStruct(block, F32),
-            jax.ShapeDtypeStruct(block, F32),
+            pltpu.VMEM((1, rows), F32),
+            pltpu.VMEM(block, F32),
+            pltpu.VMEM(block, F32),
         ),
         in_specs=[pl.BlockSpec(memory_space=pl.ANY)] * 2,
         out_specs=(pl.BlockSpec(memory_space=pltpu.VMEM),) * 3,
@@ -231,13 +252,25 @@
             pltpu.SemaphoreType.DMA((2,)),
         ],
         compiler_params=pltpu.CompilerParams(
-            collective_id=0, has_side_effects=True, vmem_limit_bytes=56 * 2**20
+            collective_id=0, has_side_effects=True, vmem_limit_bytes=40 * 2**20
         ),
         cost_estimate=pl.CostEstimate(
             flops=6 * 8 * rows * rows * width, bytes_accessed=12 * rows * width,
             transcendentals=3 * 8 * rows * rows,
         ),
     )(images, texts)
+    loss, grad_images, grad_texts = pl.pallas_call(
+        write_out,
+        out_shape=(
+            pltpu.HBM((1, rows), F32),
+            pltpu.HBM(block, F32),
+            pltpu.HBM(block, F32),
+        ),
+        in_specs=[pl.BlockSpec(memory_space=pltpu.VMEM)] * 3,
+        out_specs=(pl.BlockSpec(memory_space=pl.ANY),) * 3,
+        scratch_shapes=[pltpu.SemaphoreType.DMA((3,))],
+        compiler_params=pltpu.CompilerParams(vmem_limit_bytes=2 * 2**20),
+    )(*[pltpu.with_memory_space_constraint(r, pltpu.VMEM) for r in results])
     return loss.reshape(rows), grad_images, grad_texts
 
 

time: 95.2 us -> 85.6 us (0.90)
  local copies, waits for them, and re-layouts: 6.03 us -> 0 us
  Pallas kernels: 88.4 us -> 84.6 us
    unnamed x5 -> x0, local copies, waits for them, and re-layouts: 6.03 us -> none
    pallas_call x1 -> x2, Pallas kernels: 88.4 us -> 84.6 us  [the longest x1 82.4 us: per_device(): pl.pallas_call(kernel, out_shape=(pltpu.VMEM((1, rows), F32), pltpu.VMEM(...]
where the time goes in v2:
time: 85.6 us; the launch traced here: 85.4 us
  Pallas kernels  84.6 us (99%)
    pallas_call x1, Pallas kernels, per_device(): pl.pallas_call(kernel, out_shape=(pltpu.VMEM((1, rows), F32), pltpu.VMEM(...  82.4 us
    pallas_call x1, Pallas kernels, per_device(): pl.pallas_call(write_out, out_shape=(pltpu.HBM((1, rows), F32), pltpu.HBM...  2.21 us

profile of v2, /device:TPU:0, one launch (start us, length us, event | category | flops | bytes accessed | tf_op | source)
XLA Modules:
  0.0 85.4 jit_solution(2147373469305502053)
XLA Ops:
  0.6 82.4 %shard_map.49 = (f32[1,512]{1,0:T(1,128)S(1)}, f32[512,1152]{1,0:T(8,128)S(1)}, f32[512,1152]{1,0:T(8,128)S(1)}) custom-call(bf16[512,1152]{1,0:T(8,128)(2,1)} %images.1, bf16[512,1152]{1,0:T(8,128)(2,1)} %texts.1), custom_call_target="tpu_custom_call" | custom-call | flops 14495514624 | bytes 7077888 | tf_op jit(solution)/shard_map/pallas_call | solution.py:230
  83.1 2.2 %shard_map.50 = (f32[1,512]{1,0:T(1,128)}, f32[512,1152]{1,0:T(8,128)}, f32[512,1152]{1,0:T(8,128)}) custom-call(f32[1,512]{1,0:T(1,128)S(1)} %get-tuple-element.9.refs_0_, f32[512,1152]{1,0:T(8,128)S(1)} %get-tuple-element.10.refs_1_, f32[512,1152]{1,0:T(8,128)S(1)} %get-tuple-element.11.refs_2_), custom_call_target="tpu_custom_call" | custom-call | tf_op jit(solution)/shard_map/pallas_call | solution.py:262

commit v3 on v2

--- a/solution.py
+++ b/solution.py
@@ -14,6 +14,8 @@
 OWN, YP, AP, FAR = 0, 1, 2, 3
 CHUNK = 128
 HALF = 256
+GATHER_LAST = 384
+LAST = 320
 
 
 def pair_terms(products, scale, match):
@@ -30,6 +32,11 @@
         return (scale * sig).astype(BF16), jnp.maximum(logits, 0.0) + tail
     coef = (scale * (sig - match.astype(F32))).astype(BF16)
     return coef, jnp.maximum(jnp.where(match, -logits, logits), 0.0) + tail
+
+
+def cuts(last, rows):
+    edges = (0, CHUNK, HALF, last, rows)
+    return [pl.ds(lo, hi - lo) for lo, hi in zip(edges, edges[1:])]
 
 
 def kernel(
@@ -60,17 +67,15 @@
 
     chunks = [pl.ds(k * CHUNK, CHUNK) for k in range(rows // CHUNK)]
     image_b = [to(images.at[c], im.at[pl.ds(rows + c.start, CHUNK)], b) for c in chunks]
-    text_y = [to(texts.at[c], tx.at[YP, c], y) for c in chunks]
-    text_a = [to(texts.at[c], tx.at[AP, c], a) for c in chunks]
-    text_far = [
-        to(tx.at[AP, c], tx.at[FAR, c], y) if c.start < CHUNK else to(tx.at[YP, c], tx.at[FAR, c], a)
-        for c in chunks
-    ]
-    back_far = [
-        to(out_far.at[c], in_far.at[c], y if c.start < CHUNK else a) for c in chunks
-    ]
-    back_y = [to(out_y.at[c], in_y.at[c], y) for c in chunks]
-    back_a = [to(out_a.at[c], in_a.at[c], a) for c in chunks]
+    text_chunks, back_chunks = cuts(GATHER_LAST, rows), cuts(LAST, rows)
+    text_y = [to(texts.at[c], tx.at[YP, c], y) for c in text_chunks]
+    text_a = [to(texts.at[c], tx.at[AP, c], a) for c in text_chunks]
+    text_far = [to(tx.at[YP, c], tx.at[FAR, c], a) for c in text_chunks[:3]]
+    text_far.append(to(tx.at[AP, text_chunks[3]], tx.at[FAR, text_chunks[3]], y))
+    back_far = [to(out_far.at[c], in_far.at[c], a) for c in back_chunks[:3]]
+    back_far.append(to(out_far.at[back_chunks[3]], in_far.at[back_chunks[3]], y))
+    back_y = [to(out_y.at[c], in_y.at[c], y) for c in back_chunks]
+    back_a = [to(out_a.at[c], in_a.at[c], a) for c in back_chunks]
     back_b = [to(out_b.at[c], in_b.at[c], b) for c in chunks]
     back_loss = to(losses.at[1], far_losses, b)
 
@@ -133,75 +138,82 @@
 
     pairs(OWN, 0, rows, 0, True)
     image_b[2].wait_send()
-    start(text_a[0])
+    start(text_a[3])
     image_b[3].wait_send()
-    start(*text_a[1:])
+    arrived(text_y[0])
+    start(text_far[0])
     arrived(*image_b)
     pairs(OWN, 0, rows, 1)
+    arrived(text_y[1])
+    start(text_far[1])
     grad_texts[...] = text_part(rows)
     grad_images[...] = image_part(OWN, 0, rows, 0)
+    arrived(text_a[3])
+    start(text_far[3])
     grad_b[...] = image_part(OWN, 0, rows, 1)
 
-    arrived(text_y[0], text_y[1])
     both_pairs(YP, 0)
-    part = text_part(HALF)
-    out_y[:CHUNK] = part[:CHUNK].astype(BF16)
-    hold[CHUNK:HALF] = part[CHUNK:]
-    start(text_far[1])
+    hold[:HALF] = text_part(HALF)
+    arrived(text_y[2])
+    start(text_far[2], text_a[2])
     both_images(YP, 0)
-
-    arrived(text_a[0], text_a[1])
-    both_pairs(AP, 0)
-    part = text_part(HALF)
-    hold[:CHUNK] = part[:CHUNK]
-    out_a[CHUNK:HALF] = part[CHUNK:].astype(BF16)
-    both_images(AP, 0)
-
-    arrived(text_y[2])
-    start(text_far[2], text_far[0])
-    arrived(text_y[3])
-    start(text_far[3])
-    both_pairs(YP, HALF)
-    hold[HALF:] = text_part(HALF)
-    both_images(YP, HALF)
-
-    arrived(text_a[2], text_a[3])
-    both_pairs(AP, HALF)
-    out_a[HALF:] = text_part(HALF).astype(BF16)
-    start(back_y[0])
-    both_images(AP, HALF)
 
     arrived(text_far[0], text_far[1])
     both_pairs(FAR, 0)
+    start(text_a[0])
     out_far[:HALF] = text_part(HALF).astype(BF16)
-    start(back_far[1], back_far[0])
+    start(text_a[1])
     both_images(FAR, 0)
+
     arrived(text_far[2], text_far[3])
-    start(back_a[1], back_a[2])
     both_pairs(FAR, HALF)
-    start(back_loss)
     out_far[HALF:] = text_part(HALF).astype(BF16)
-    start(back_far[2], back_far[3])
-    out_b[...] = (grad_b[...] + image_part(FAR, HALF, HALF, 1)).astype(BF16)
-    grad_images[...] += image_part(FAR, HALF, HALF, 0)
+    start(back_far[3], back_far[0])
+    both_images(FAR, HALF)
+
+    arrived(text_a[2])
+    both_pairs(AP, HALF)
+    part = text_part(HALF)
+    out_a[HALF:LAST] = part[:LAST - HALF].astype(BF16)
+    hold[LAST:] = part[LAST - HALF:]
+    start(back_far[1], back_far[2])
+    both_images(AP, HALF)
+
+    arrived(text_y[3])
+    both_pairs(YP, HALF)
+    part = text_part(HALF)
+    hold[HALF:LAST] = part[:LAST - HALF]
+    out_y[LAST:] = part[LAST - HALF:].astype(BF16)
+    start(back_y[3], back_a[2])
+    both_images(YP, HALF)
 
     def pass_on(k):
-        out, back = (out_a, back_a) if k == 0 else (out_y, back_y)
-        c = chunks[k]
+        out, back = (out_a, back_a) if k == 3 else (out_y, back_y)
+        c = back_chunks[k]
         arrived(back_far[k])
         out[c] = (hold[c] + in_far[c].astype(F32)).astype(BF16)
         start(back[k])
 
+    arrived(text_a[0], text_a[1])
+    both_pairs(AP, 0)
+    start(back_loss)
+    pass_on(0)
+    out_a[:HALF] = text_part(HALF).astype(BF16)
+    start(back_a[0])
+    out_b[...] = (grad_b[...] + image_part(AP, 0, HALF, 1)).astype(BF16)
+    start(back_b[0], back_a[1])
     pass_on(1)
-    start(back_a[3], back_b[0])
+    start(back_b[1])
+    grad_images[...] += image_part(AP, 0, HALF, 0)
     pass_on(2)
-    start(*back_b[1:])
+    start(back_b[2])
     pass_on(3)
-    pass_on(0)
+    start(back_b[3])
+
     arrived(back_loss)
     row_loss[...] = jnp.sum(losses[0] + far_losses[...], axis=0, keepdims=True) * (1.0 / (8 * rows))
-    for k in (1, 2, 3, 0):
-        c = chunks[k]
+    for k in range(4):
+        c = back_chunks[k]
         arrived(back_a[k], back_y[k])
         grad_texts[c] += in_a[c].astype(F32) + in_y[c].astype(F32)
     for k, c in enumerate(chunks):

time: 85.6 us -> 82.7 us (0.966)
  Pallas kernels: 84.6 us -> 81.6 us
    pallas_call x1, Pallas kernels: 82.4 us -> 79.4 us  [per_device(): pl.pallas_call(kernel, out_shape=(pltpu.VMEM((1, rows), F32), pltpu.VMEM(...]
where the time goes in v3:
time: 82.7 us; the launch traced here: 82.4 us
  Pallas kernels  81.6 us (99%)
    pallas_call x1, Pallas kernels, per_device(): pl.pallas_call(kernel, out_shape=(pltpu.VMEM((1, rows), F32), pltpu.VMEM(...  79.4 us
    pallas_call x1, Pallas kernels, per_device(): pl.pallas_call(write_out, out_shape=(pltpu.HBM((1, rows), F32), pltpu.HBM...  2.21 us

profile of v3, /device:TPU:0, one launch (start us, length us, event | category | flops | bytes accessed | tf_op | source)
XLA Modules:
  0.0 82.4 jit_solution(11114769676739650591)
XLA Ops:
  0.6 79.4 %shard_map.49 = (f32[1,512]{1,0:T(1,128)S(1)}, f32[512,1152]{1,0:T(8,128)S(1)}, f32[512,1152]{1,0:T(8,128)S(1)}) custom-call(bf16[512,1152]{1,0:T(8,128)(2,1)} %images.1, bf16[512,1152]{1,0:T(8,128)(2,1)} %texts.1), custom_call_target="tpu_custom_call" | custom-call | flops 14495514624 | bytes 7077888 | tf_op jit(solution)/shard_map/pallas_call | solution.py:242
  80.0 2.2 %shard_map.50 = (f32[1,512]{1,0:T(1,128)}, f32[512,1152]{1,0:T(8,128)}, f32[512,1152]{1,0:T(8,128)}) custom-call(f32[1,512]{1,0:T(1,128)S(1)} %get-tuple-element.9.refs_0_, f32[512,1152]{1,0:T(8,128)S(1)} %get-tuple-element.10.refs_1_, f32[512,1152]{1,0:T(8,128)S(1)} %get-tuple-element.11.refs_2_), custom_call_target="tpu_custom_call" | custom-call | tf_op jit(solution)/shard_map/pallas_call | solution.py:274

commit v4 on v3

--- a/solution.py
+++ b/solution.py
@@ -14,8 +14,7 @@
 OWN, YP, AP, FAR = 0, 1, 2, 3
 CHUNK = 128
 HALF = 256
-GATHER_LAST = 384
-LAST = 320
+FIRST = 224
 
 
 def pair_terms(products, scale, match):
@@ -34,8 +33,7 @@
     return coef, jnp.maximum(jnp.where(match, -logits, logits), 0.0) + tail
 
 
-def cuts(last, rows):
-    edges = (0, CHUNK, HALF, last, rows)
+def cuts(*edges):
     return [pl.ds(lo, hi - lo) for lo, hi in zip(edges, edges[1:])]
 
 
@@ -67,18 +65,23 @@
 
     chunks = [pl.ds(k * CHUNK, CHUNK) for k in range(rows // CHUNK)]
     image_b = [to(images.at[c], im.at[pl.ds(rows + c.start, CHUNK)], b) for c in chunks]
-    text_chunks, back_chunks = cuts(GATHER_LAST, rows), cuts(LAST, rows)
+    text_chunks = cuts(0, CHUNK, HALF, HALF + CHUNK, rows)
+    back_chunks = cuts(0, FIRST, HALF, HALF + CHUNK, rows)
     text_y = [to(texts.at[c], tx.at[YP, c], y) for c in text_chunks]
     text_a = [to(texts.at[c], tx.at[AP, c], a) for c in text_chunks]
     text_far = [to(tx.at[YP, c], tx.at[FAR, c], a) for c in text_chunks[:3]]
     text_far.append(to(tx.at[AP, text_chunks[3]], tx.at[FAR, text_chunks[3]], y))
-    back_far = [to(out_far.at[c], in_far.at[c], a) for c in back_chunks[:3]]
-    back_far.append(to(out_far.at[back_chunks[3]], in_far.at[back_chunks[3]], y))
+    back_far = [to(out_far.at[back_chunks[0]], in_far.at[back_chunks[0]], y)]
+    back_far += [to(out_far.at[c], in_far.at[c], a) for c in back_chunks[1:]]
     back_y = [to(out_y.at[c], in_y.at[c], y) for c in back_chunks]
     back_a = [to(out_a.at[c], in_a.at[c], a) for c in back_chunks]
     back_b = [to(out_b.at[c], in_b.at[c], b) for c in chunks]
     back_loss = to(losses.at[1], far_losses, b)
 
+    own_text = pltpu.make_async_copy(texts, tx.at[OWN], local.at[0])
+    own_image = pltpu.make_async_copy(images, im.at[pl.ds(0, rows)], local.at[1])
+    own_text.start()
+    own_image.start()
     barrier = pltpu.get_barrier_semaphore()
     for device in (a, b, y):
         pl.semaphore_signal(barrier, inc=1, device_id=(device,), device_id_type=MESH)
@@ -96,64 +99,82 @@
             copy.wait_recv()
 
     start(*image_b, *text_y)
-    own_text = pltpu.make_async_copy(texts, tx.at[OWN], local.at[0])
-    own_image = pltpu.make_async_copy(images, im.at[pl.ds(0, rows)], local.at[1])
-    own_text.start()
-    own_image.start()
     own_text.wait()
     own_image.wait()
 
-    def pairs(slot, first, size, side, diagonal=False):
-        columns = pl.ds(side * rows, rows)
+    def own_pairs(first, size):
+        columns = slice(first, first + size)
         products = lax.dot_general(
-            tx[slot, first:first + size], im[columns], (((1,), (1,)), ((), ())),
+            tx[OWN], im[columns], (((1,), (1,)), ((), ())), preferred_element_type=F32
+        )
+        match = None
+        if first == 0:
+            match = lax.broadcasted_iota(jnp.int32, (rows, size), 0) == (
+                lax.broadcasted_iota(jnp.int32, (rows, size), 1)
+            )
+        c, loss = pair_terms(products, scale, match)
+        coef[:, columns] = c
+        side, at = divmod(first, rows)
+        losses[side, :, at:at + size] = loss.reshape(rows // 8, 8, size).sum(0)
+
+    def text_part(size):
+        return jnp.dot(coef[:size], im[...], preferred_element_type=F32)
+
+    def image_part(slot, columns, first=0):
+        size = rows if slot == OWN else HALF
+        return lax.dot_general(
+            coef[:size, columns], tx[slot, first:first + size],
+            (((0,), (0,)), ((), ())), preferred_element_type=F32,
+        )
+
+    def both_pairs(slot, first):
+        products = lax.dot_general(
+            tx[slot, first:first + HALF], im[...], (((1,), (1,)), ((), ())),
             preferred_element_type=F32,
         )
-        match = None
-        if diagonal:
-            match = lax.broadcasted_iota(jnp.int32, (size, rows), 0) == (
-                lax.broadcasted_iota(jnp.int32, (size, rows), 1)
-            )
-        c, loss = pair_terms(products, scale, match)
-        coef[:size, columns] = c
-        part = loss.reshape(size // 8, 8, rows).sum(0)
-        losses[side] = part if slot == OWN else losses[side] + part
-
-    def text_part(size):
-        return jnp.dot(coef[:size], im[...], preferred_element_type=F32)
-
-    def image_part(slot, first, size, side):
-        return lax.dot_general(
-            coef[:size, side * rows:(side + 1) * rows], tx[slot, first:first + size],
-            (((0,), (0,)), ((), ())), preferred_element_type=F32,
-        )
-
-    def both_pairs(slot, first):
-        pairs(slot, first, HALF, 0)
-        pairs(slot, first, HALF, 1)
+        c, loss = pair_terms(products, scale, None)
+        coef[:HALF] = c
+        part = loss.reshape(HALF // 8, 8, 2 * rows).sum(0)
+        losses[0] += part[:, :rows]
+        losses[1] += part[:, rows:]
 
     def both_images(slot, first):
-        grad_images[...] += image_part(slot, first, HALF, 0)
-        grad_b[...] += image_part(slot, first, HALF, 1)
-
-    pairs(OWN, 0, rows, 0, True)
+        part = image_part(slot, slice(None), first)
+        grad_images[...] += part[:rows]
+        grad_b[...] += part[rows:]
+
+    def own(first, size):
+        columns = slice(first, first + size)
+        part = image_part(OWN, columns)
+        if first < rows:
+            grad_images[...] = part
+        else:
+            grad_b[first - rows:first - rows + size] = part
+        part = jnp.dot(coef[:, columns], im[columns], preferred_element_type=F32)
+        grad_texts[...] = part if first == 0 else grad_texts[...] + part
+
+    own_pairs(0, rows)
+    own(0, rows)
+    arrived(image_b[0], image_b[1])
+    own_pairs(rows, HALF)
     image_b[2].wait_send()
     start(text_a[3])
+    own(rows, HALF)
     image_b[3].wait_send()
     arrived(text_y[0])
     start(text_far[0])
-    arrived(*image_b)
-    pairs(OWN, 0, rows, 1)
+    arrived(image_b[2], image_b[3])
+    own_pairs(rows + HALF, HALF)
     arrived(text_y[1])
     start(text_far[1])
-    grad_texts[...] = text_part(rows)
-    grad_images[...] = image_part(OWN, 0, rows, 0)
+    own(rows + HALF, HALF)
     arrived(text_a[3])
     start(text_far[3])
-    grad_b[...] = image_part(OWN, 0, rows, 1)
 
     both_pairs(YP, 0)
-    hold[:HALF] = text_part(HALF)
+    part = text_part(HALF)
+    out_y[:FIRST] = part[:FIRST].astype(BF16)
+    hold[FIRST:HALF] = part[FIRST:]
     arrived(text_y[2])
     start(text_far[2], text_a[2])
     both_images(YP, 0)
@@ -166,29 +187,28 @@
     both_images(FAR, 0)
 
     arrived(text_far[2], text_far[3])
+    start(back_far[0])
     both_pairs(FAR, HALF)
     out_far[HALF:] = text_part(HALF).astype(BF16)
-    start(back_far[3], back_far[0])
+    start(back_far[1], back_far[2])
     both_images(FAR, HALF)
 
     arrived(text_a[2])
+    start(back_y[0])
     both_pairs(AP, HALF)
-    part = text_part(HALF)
-    out_a[HALF:LAST] = part[:LAST - HALF].astype(BF16)
-    hold[LAST:] = part[LAST - HALF:]
-    start(back_far[1], back_far[2])
+    start(back_far[3])
+    out_a[HALF:] = text_part(HALF).astype(BF16)
     both_images(AP, HALF)
 
     arrived(text_y[3])
     both_pairs(YP, HALF)
-    part = text_part(HALF)
-    hold[HALF:LAST] = part[:LAST - HALF]
-    out_y[LAST:] = part[LAST - HALF:].astype(BF16)
-    start(back_y[3], back_a[2])
+    start(back_a[2])
+    hold[HALF:] = text_part(HALF)
+    start(back_a[3])
     both_images(YP, HALF)
 
     def pass_on(k):
-        out, back = (out_a, back_a) if k == 3 else (out_y, back_y)
+        out, back = (out_a, back_a) if k == 0 else (out_y, back_y)
         c = back_chunks[k]
         arrived(back_far[k])
         out[c] = (hold[c] + in_far[c].astype(F32)).astype(BF16)
@@ -197,17 +217,19 @@
     arrived(text_a[0], text_a[1])
     both_pairs(AP, 0)
     start(back_loss)
+    pass_on(1)
+    part = text_part(HALF)
+    out_a[FIRST:HALF] = part[FIRST:].astype(BF16)
+    hold[:FIRST] = part[:FIRST]
+    start(back_a[1])
+    out_b[...] = (grad_b[...] + image_part(AP, slice(rows, None))).astype(BF16)
+    start(back_b[0])
+    pass_on(2)
+    start(back_b[1])
+    grad_images[...] += image_part(AP, slice(0, rows))
+    pass_on(3)
+    start(back_b[2])
     pass_on(0)
-    out_a[:HALF] = text_part(HALF).astype(BF16)
-    start(back_a[0])
-    out_b[...] = (grad_b[...] + image_part(AP, 0, HALF, 1)).astype(BF16)
-    start(back_b[0], back_a[1])
-    pass_on(1)
-    start(back_b[1])
-    grad_images[...] += image_part(AP, 0, HALF, 0)
-    pass_on(2)
-    start(back_b[2])
-    pass_on(3)
     start(back_b[3])
 
     arrived(back_loss)
@@ -226,7 +248,11 @@
 
 def write_out(*refs):
     sources, targets, done = refs[:3], refs[3:6], refs[6]
-    copies = [pltpu.make_async_copy(s, t, done.at[k]) for k, (s, t) in enumerate(zip(sources, targets))]
+    rows = sources[1].shape[0]
+    copies = [pltpu.make_async_copy(sources[0], targets[0], done.at[0])]
+    for k in range(8):
+        which, part = 1 + k % 2, pl.ds(k // 2 * (rows // 4), rows // 4)
+        copies.append(pltpu.make_async_copy(sources[which].at[part], targets[which].at[part], done.at[1 + k]))
     for copy in copies:
         copy.start()
     for copy in copies:
@@ -280,7 +306,7 @@
         ),
         in_specs=[pl.BlockSpec(memory_space=pltpu.VMEM)] * 3,
         out_specs=(pl.BlockSpec(memory_space=pl.ANY),) * 3,
-        scratch_shapes=[pltpu.SemaphoreType.DMA((3,))],
+        scratch_shapes=[pltpu.SemaphoreType.DMA((9,))],
         compiler_params=pltpu.CompilerParams(vmem_limit_bytes=2 * 2**20),
     )(*[pltpu.with_memory_space_constraint(r, pltpu.VMEM) for r in results])
     return loss.reshape(rows), grad_images, grad_texts

time: 82.7 us -> 80.2 us (0.970)
  Pallas kernels: 81.6 us -> 78.6 us
    pallas_call x1, Pallas kernels: 79.4 us -> 76.3 us  [per_device(): pl.pallas_call(kernel, out_shape=(pltpu.VMEM((1, rows), F32), pltpu.VMEM(...]
where the time goes in v4:
time: 80.2 us; the launch traced here: 79.4 us
  Pallas kernels  78.6 us (98%)
    pallas_call x1, Pallas kernels, per_device(): pl.pallas_call(kernel, out_shape=(pltpu.VMEM((1, rows), F32), pltpu.VMEM(...  76.3 us
    pallas_call x1, Pallas kernels, per_device(): pl.pallas_call(write_out, out_shape=(pltpu.HBM((1, rows), F32), pltpu.HBM...  2.26 us

profile of v4, /device:TPU:0, one launch (start us, length us, event | category | flops | bytes accessed | tf_op | source)
XLA Modules:
  0.0 79.4 jit_solution(18392002119711388509)
XLA Ops:
  0.6 76.3 %shard_map.49 = (f32[1,512]{1,0:T(1,128)S(1)}, f32[512,1152]{1,0:T(8,128)S(1)}, f32[512,1152]{1,0:T(8,128)S(1)}) custom-call(bf16[512,1152]{1,0:T(8,128)(2,1)} %images.1, bf16[512,1152]{1,0:T(8,128)(2,1)} %texts.1), custom_call_target="tpu_custom_call" | custom-call | flops 14495514624 | bytes 7077888 | tf_op jit(solution)/shard_map/pallas_call | solution.py:268
  77.0 2.3 %shard_map.50 = (f32[1,512]{1,0:T(1,128)}, f32[512,1152]{1,0:T(8,128)}, f32[512,1152]{1,0:T(8,128)}) custom-call(f32[1,512]{1,0:T(1,128)S(1)} %get-tuple-element.9.refs_0_, f32[512,1152]{1,0:T(8,128)S(1)} %get-tuple-element.10.refs_1_, f32[512,1152]{1,0:T(8,128)S(1)} %get-tuple-element.11.refs_2_), custom_call_target="tpu_custom_call" | custom-call | tf_op jit(solution)/shard_map/pallas_call | solution.py:300

commit v5 on v4

--- a/solution.py
+++ b/solution.py
@@ -158,11 +158,10 @@
     arrived(image_b[0], image_b[1])
     own_pairs(rows, HALF)
     image_b[2].wait_send()
-    start(text_a[3])
+    arrived(text_y[0])
+    start(text_a[3], text_far[0])
     own(rows, HALF)
     image_b[3].wait_send()
-    arrived(text_y[0])
-    start(text_far[0])
     arrived(image_b[2], image_b[3])
     own_pairs(rows + HALF, HALF)
     arrived(text_y[1])
@@ -190,13 +189,12 @@
     start(back_far[0])
     both_pairs(FAR, HALF)
     out_far[HALF:] = text_part(HALF).astype(BF16)
-    start(back_far[1], back_far[2])
+    start(back_far[1], back_far[2], back_far[3])
     both_images(FAR, HALF)
 
     arrived(text_a[2])
     start(back_y[0])
     both_pairs(AP, HALF)
-    start(back_far[3])
     out_a[HALF:] = text_part(HALF).astype(BF16)
     both_images(AP, HALF)
 
@@ -226,11 +224,11 @@
     start(back_b[0])
     pass_on(2)
     start(back_b[1])
-    grad_images[...] += image_part(AP, slice(0, rows))
     pass_on(3)
     start(back_b[2])
     pass_on(0)
     start(back_b[3])
+    grad_images[...] += image_part(AP, slice(0, rows))
 
     arrived(back_loss)
     row_loss[...] = jnp.sum(losses[0] + far_losses[...], axis=0, keepdims=True) * (1.0 / (8 * rows))

time: 80.2 us -> 80.2 us (level)
  no operation moved by 1% of the time
where the time goes in v5:
time: 80.2 us; the launch traced here: 79.4 us
  Pallas kernels  78.6 us (98%)
    pallas_call x1, Pallas kernels, per_device(): pl.pallas_call(kernel, out_shape=(pltpu.VMEM((1, rows), F32), pltpu.VMEM(...  76.3 us
    pallas_call x1, Pallas kernels, per_device(): pl.pallas_call(write_out, out_shape=(pltpu.HBM((1, rows), F32), pltpu.HBM...  2.26 us

profile of v5, /device:TPU:0, one launch (start us, length us, event | category | flops | bytes accessed | tf_op | source)
XLA Modules:
  0.0 79.4 jit_solution(17372242184351811950)
XLA Ops:
  0.6 76.3 %shard_map.49 = (f32[1,512]{1,0:T(1,128)S(1)}, f32[512,1152]{1,0:T(8,128)S(1)}, f32[512,1152]{1,0:T(8,128)S(1)}) custom-call(bf16[512,1152]{1,0:T(8,128)(2,1)} %images.1, bf16[512,1152]{1,0:T(8,128)(2,1)} %texts.1), custom_call_target="tpu_custom_call" | custom-call | flops 14495514624 | bytes 7077888 | tf_op jit(solution)/shard_map/pallas_call | solution.py:266
  77.0 2.3 %shard_map.50 = (f32[1,512]{1,0:T(1,128)}, f32[512,1152]{1,0:T(8,128)}, f32[512,1152]{1,0:T(8,128)}) custom-call(f32[1,512]{1,0:T(1,128)S(1)} %get-tuple-element.9.refs_0_, f32[512,1152]{1,0:T(8,128)S(1)} %get-tuple-element.10.refs_1_, f32[512,1152]{1,0:T(8,128)S(1)} %get-tuple-element.11.refs_2_), custom_call_target="tpu_custom_call" | custom-call | tf_op jit(solution)/shard_map/pallas_call | solution.py:298
